TPU v7x, 256 devices: a whole 4x4x8 slice. The times are simulated.
256 devices in a mesh: dp: 64 (over y, z, core), tensor: 4 (over x).
Axes of the slice: x: 4, y: 4, z: 8, core: 2. Of those that a mesh axis runs over, the one named last changes fastest.
Arguments:
- gradient: bfloat16 [64, 128, 49152], P('dp', None, 'tensor'), may hold values from -12 to 12, as said below
- error_buffer: bfloat16 [64, 128, 49152], P('dp', None, 'tensor'), may hold values from -3 to 3
- q_prev: float32 [16, 49152], P(None, 'tensor'), may hold values from -6 to 6
Outputs:
- p_basis: float32 [128, 16], replicated
- q_new: float32 [16, 49152], P(None, 'tensor')
- residual: bfloat16 [64, 128, 49152], P('dp', None, 'tensor')
Inputs may be any that keep to these rules, and one draw needn't show every extreme that they name: Each row of each replica's gradient carries its own scale, between 0.3 and 3.
All inputs are finite; a program needn't handle non-finite values.
Results may differ from a plain program's by a relative error of at most 0.001.
Values sent between devices are 32-bit elements; how exact they have to be, the bound alone decides.
A program may use at most 64 MiB of HBM per device.

v0:
```python
import jax
import jax.numpy as jnp
from jax import lax
from jax.sharding import PartitionSpec as P

PRECISE = lax.Precision.HIGHEST


def orthonormal(p_total):
    gram_matrix = jnp.dot(p_total.T, p_total, precision=PRECISE)
    factor = jnp.linalg.cholesky(gram_matrix)
    return jax.scipy.linalg.solve_triangular(factor, p_total.T, lower=True).T


def shards(gradient, error_buffer, q_prev):
    merged = gradient[0].astype(jnp.float32) + error_buffer[0].astype(jnp.float32)
    partial_value = lax.dot_general(merged, q_prev, (((1,), (1,)), ((), ())), precision=PRECISE)
    across = lax.psum(partial_value, "tensor")
    p_total = lax.psum(across, "dp")
    p_basis = orthonormal(p_total)
    local_q = lax.dot_general(p_basis, merged, (((0,), (0,)), ((), ())), precision=PRECISE)
    replicas = lax.axis_size("dp")
    q_new = lax.psum(local_q, "dp") / replicas
    update = jnp.dot(p_basis, q_new, precision=PRECISE)
    residual = (merged - update).astype(jnp.bfloat16)
    return (p_basis, q_new, residual[None])


def solution(mesh):
    return jax.shard_map(
        shards,
        mesh=mesh,
        in_specs=(P("dp", None, "tensor"), P("dp", None, "tensor"), P(None, "tensor")),
        out_specs=(P(), P(None, "tensor"), P("dp", None, "tensor")),
        check_vma=False,
    )
```

profile of v0, /device:TPU:1, one launch (start us, length us, event | category | flops | bytes accessed | tf_op | source)
XLA Modules:
  0.0 360.7 jit_solution(14741537136246855192)
XLA Ops:
  7.2 0.0 copy-start
  7.2 0.0 all-reduce.2.cloned.1.call-start
  7.2 1.1 copy-done
  8.3 7.2 %fusion.4 = f32[128,16]{0,1:T(8,128)S(1)} fusion(f32[16,12288]{1,0:T(8,128)S(1)} %copy-done, bf16[1,128,12288]{2,1,0:T(8,128)(2,1)} %param.4, bf16[1,128,12288]{2,1,0:T(8,128)(2,1)} %param.3), kind=kOutput, calls=%fused_computation.5 | convolution fusion | flops 306708480 | bytes 7086080 | tf_op jit(solution)/shard_map/dot_general | solution.py:17
  15.5 9.4 %psum.21 = f32[128,16]{0,1:T(8,128)S(1)} all-reduce(f32[128,16]{0,1:T(8,128)S(1)} %fusion.4), channel_id=1, replica_groups=mesh['dp'=64,'tensor'=4] {'tensor'}, use_global_device_ids=true, to_apply=%region_0.0 | all-reduce | flops 2048 | bytes 16384 | tf_op jit(solution)/shard_map/psum | solution.py:18
  25.0 131.5 %psum.22 = f32[128,16]{0,1:T(8,128)S(1)} all-reduce(f32[128,16]{0,1:T(8,128)S(1)} %psum.21), channel_id=1, replica_groups=mesh['dp'=64,'tensor'=4] {'dp'}, use_global_device_ids=true, to_apply=%region_1.0 | all-reduce | flops 2048 | bytes 16384 | tf_op jit(solution)/shard_map/psum | solution.py:19
  156.4 0.1 fusion.10
  156.6 0.1 copy.6
  156.6 1.5 cholesky.16
  158.1 0.6 compare_reduce_fusion
  158.8 0.6 fusion.6
  159.4 1.2 custom-call.7
  160.7 0.2 fusion.7
  160.9 0.0 copy-start.2
  160.9 6.3 %fusion.2 = f32[16,12288]{1,0:T(8,128)} fusion(f32[16,128]{1,0:T(8,128)S(1)} %fusion.7, bf16[1,128,12288]{2,1,0:T(8,128)(2,1)} %param.4, bf16[1,128,12288]{2,1,0:T(8,128)(2,1)} %param.3), kind=kOutput, calls=%fused_computation.3 | convolution fusion | flops 306708480 | bytes 7086080 | tf_op jit(solution)/shard_map/dot_general | solution.py:21
  167.2 0.0 all-reduce.2.cloned.1.call-update
  167.3 176.3 %all-reduce.2.cloned.1.call-done = f32[16,12288]{1,0:T(8,128)} async-done(((f32[16,12288]{1,0:T(8,128)}), f32[16,12288]{1,0:T(8,128)}) %all-reduce.2.cloned.1.call-update) | async-done | bytes 786448 | tf_op jit(solution)/shard_map/psum | solution.py:23
  343.6 1.2 broadcast_multiply_fusion
  344.8 0.0 copy-done.2
  344.8 0.0 copy-start.1
  344.8 9.1 %fusion.1 = bf16[1,128,12288]{2,1,0:T(8,128)(2,1)} fusion(f32[16,128]{1,0:T(8,128)S(1)} %fusion.7, f32[16,12288]{1,0:T(8,128)S(1)} %broadcast_multiply_fusion, bf16[1,128,12288]{2,1,0:T(8,128)(2,1)} %param.4, bf16[1,128,12288]{2,1,0:T(8,128)(2,1)} %param.3), kind=kOutput, calls=%fused_computation.2 | convolution fusion | flops 309854208 | bytes 10231808 | tf_op jit(solution)/shard_map/dot_general | solution.py:24
  353.9 0.0 copy-done.1
  (2 shorter events, 0.0 us)
Async XLA Ops:
  7.2 1.1 copy-start
  7.2 336.4 %all-reduce.2.cloned.1.call-start = ((), (), s32[]{:S(2)}) async-start(), calls=%async_computation | async-start | bytes 1572864 | tf_op jit(solution)/shard_map/psum | solution.py:23
  160.9 183.9 %copy-start.2 = (f32[16,128]{1,0:T(8,128)}, f32[16,128]{1,0:T(8,128)S(1)}, u32[]{:S(2)}) copy-start(f32[16,128]{1,0:T(8,128)S(1)} %fusion.7) | copy-start | bytes 24580
  344.8 9.1 %copy-start.1 = (f32[16,12288]{1,0:T(8,128)}, f32[16,12288]{1,0:T(8,128)S(1)}, u32[]{:S(2)}) copy-start(f32[16,12288]{1,0:T(8,128)S(1)} %broadcast_multiply_fusion) | copy-start | bytes 2359300
Sparse Core Ops, SparseCore 0:
  167.4 176.1 all-reduce.1
where the time goes:
time: 362 us; the launch traced here: 361 us
  waiting for transfers between devices  176 us (49%)
  blocking collectives  141 us (39%)
  matrix products  23 us (6%)
  between operations  14.1 us (4%)
  other arithmetic  5.21 us (1%)
    psum x1, waiting for transfers between devices, shards(): q_new = lax.psum(local_q, 'dp') / replicas  176 us
    psum x1, blocking collectives, shards(): p_total = lax.psum(across, 'dp')  131 us
    psum x1, blocking collectives, shards(): across = lax.psum(partial_value, 'tensor')  9.41 us
    dot_general x1, matrix products, shards(): update = jnp.dot(p_basis, q_new, precision=PRECISE)  9.1 us
  transfers between devices with their start and end apart: 1, of which 1 were waited for; matrix products, arithmetic and copies ran while one was open for 0% of the time, Pallas kernels for 0%

commit v1 on v0

v1 whole, which is shorter than its diff:
```python
import functools

import jax
import jax.numpy as jnp
from jax import lax
from jax.experimental import pallas as pl
from jax.experimental.pallas import tpu as pltpu
from jax.sharding import PartitionSpec as P

MESH = pl.DeviceIdType.MESH
F32 = jnp.float32
BF16 = jnp.bfloat16

NX, NY, NZ, NC = 4, 4, 8, 2
FAR = [4, 3, 5, 2, 6, 1, 7]
NEAR = FAR[::-1]
DYS = [2, 1, 3]


def position():
    dp, x = lax.axis_index("dp"), lax.axis_index("tensor")
    c = lax.rem(dp, NC)
    z = lax.rem(lax.div(dp, NC), NZ)
    y = lax.div(dp, NC * NZ)
    return x, y, z, c


def device(x, y, z, c):
    return ((y * NZ + z) * NC + c, x)


def parts_of(value, n):
    out = []
    for _ in range(n):
        part = value.astype(BF16)
        out.append(part)
        value = value - part.astype(F32)
    return out


def orthonormal_rows(pt):
    rank = pt.shape[0]
    gram = [
        jnp.broadcast_to(jnp.sum(pt * pt[k : k + 1], axis=1, keepdims=True), pt.shape)
        for k in range(rank)
    ]
    row = lax.broadcasted_iota(jnp.int32, pt.shape, 0)
    rows = []
    for k in range(rank):
        pivot = gram[k][k : k + 1]
        root = lax.rsqrt(pivot)
        root = root * (1.5 - 0.5 * pivot * root * root)
        factor = gram[k] * root
        basis = pt[k : k + 1] * root
        rows.append(basis)
        pt = pt - factor * basis
        for j in range(k + 1, rank):
            gram[j] = gram[j] - factor * factor[j : j + 1]
    del row
    return jnp.concatenate(rows, axis=0)


def reduce_kernel(
    g_hbm, e_hbm, q_hbm, pt_out, qn_out,
    ge, qprev, pcore, pz, pxy, psend, qloc, crecv, hs, yrecv, zs, zrecv, qn,
    load_sem, pc_sem, pz_sem, pxy_sem, c_sem, y_sem, z_sem, az_sem, ay_sem, ac_sem, out_sem,
):
    x, y, z, c = position()
    cols = q_hbm.shape[1]
    rows = g_hbm.shape[1]
    rank = q_hbm.shape[0]
    half = rank // NC
    unit = cols // (NY * NZ)
    group = NY * unit
    pending = []

    def send(src, dst, sems, index, to):
        copy = pltpu.make_async_remote_copy(
            src_ref=src, dst_ref=dst, send_sem=sems.at[(0,) + index], recv_sem=sems.at[(1,) + index],
            device_id=to, device_id_type=MESH,
        )
        copy.start()
        pending.append(copy)
        return copy

    loads = []
    for k in range(NZ):
        s = pl.ds(k * group, group)
        batch = [
            pltpu.make_async_copy(q_hbm.at[:, s], qprev.at[:, s], load_sem.at[k, 0]),
            pltpu.make_async_copy(g_hbm.at[0, :, s], ge.at[pl.ds(0, rows), s], load_sem.at[k, 1]),
            pltpu.make_async_copy(e_hbm.at[0, :, s], ge.at[pl.ds(rows, rows), s], load_sem.at[k, 2]),
        ]
        for copy in batch:
            copy.start()
        loads.append(batch)

    other = device(x, y, z, 1 - c)
    z_peer = {d: device(x, y, lax.rem(z + d, NZ), c) for d in range(1, NZ)}
    xy_peer = {
        (dx, dy): device(lax.rem(x + dx, NX), lax.rem(y + dy, NY), z, c)
        for dx in range(NX) for dy in range(NY) if (dx, dy) != (0, 0)
    }
    barrier = pltpu.get_barrier_semaphore()
    everyone = [other, *z_peer.values(), *xy_peer.values()]
    for peer in everyone:
        pl.semaphore_signal(barrier, inc=1, device_id=peer, device_id_type=MESH)

    total = jnp.zeros((3 * rank, 2 * rows), F32)
    for k in range(NZ):
        for copy in loads[k]:
            copy.wait()
        s = pl.ds(k * group, group)
        stack = jnp.concatenate(parts_of(qprev[:, s], 3), axis=0)
        total += lax.dot_general(stack, ge[:, s], (((1,), (1,)), ((), ())), preferred_element_type=F32)
    total = total[:, :rows] + total[:, rows:]
    mine = total[:rank] + total[rank : 2 * rank] + total[2 * rank :]

    pl.semaphore_wait(barrier, len(everyone))

    psend[0] = mine
    send(psend.at[0], pcore, pc_sem, (), other).wait_recv()
    mine = mine + pcore[...]
    psend[1] = mine
    pz[z] = mine
    copies = [send(psend.at[1], pz.at[z], pz_sem, (d,), z_peer[d]) for d in FAR]
    for copy in copies:
        copy.wait_recv()
    mine = pz[0]
    for k in range(1, NZ):
        mine = mine + pz[k]
    psend[2] = mine
    slot = y * NX + x
    pxy[slot] = mine
    order = sorted(xy_peer, key=lambda d: -(min(d[0], NX - d[0]) + min(d[1], NY - d[1])))
    copies = [send(psend.at[2], pxy.at[slot], pxy_sem, d, xy_peer[d]) for d in order]
    for copy in copies:
        copy.wait_recv()
    mine = pxy[0]
    for k in range(1, NX * NY):
        mine = mine + pxy[k]

    basis = orthonormal_rows(mine)
    pt_out[...] = basis
    stack = jnp.concatenate(parts_of(basis, 3), axis=0)
    stack = jnp.concatenate([stack, stack], axis=1)

    order = FAR + [0]
    copies = {}
    for d in order:
        s = pl.ds(pl.multiple_of(lax.rem(z + d, NZ) * group, group), group)
        three = jnp.dot(stack, ge[:, s], preferred_element_type=F32)
        local = three[:rank] + three[rank : 2 * rank] + three[2 * rank :]
        qloc[d, 0] = local[:half]
        qloc[d, 1] = local[half:]
        copies[d] = send(qloc.at[d, 1 - c], crecv.at[d], c_sem, (d,), other)
    y_copies = {}
    for d in order:
        copies[d].wait_recv()
        both = qloc[d, c] + crecv[d]
        for k in range(NY):
            hs[d, k] = both[:, k * unit : (k + 1) * unit]
        y_copies[d] = [
            send(hs.at[d, lax.rem(y + dy, NY)], yrecv.at[d, dy], y_sem, (d, dy), xy_peer[0, dy]) for dy in DYS
        ]
    z_copies = []
    for d in order:
        for copy in y_copies[d]:
            copy.wait_recv()
        value = hs[d, y] + yrecv[d, 1] + yrecv[d, 2] + yrecv[d, 3]
        if d:
            zs[d] = value
            z_copies.append(send(zs.at[d], zrecv.at[d], z_sem, (d,), z_peer[d]))
    for copy in z_copies:
        copy.wait_recv()
    for d in range(1, NZ):
        value = value + zrecv[d]
    value = value * (1.0 / (NY * NZ * NC))

    def place(ty, tz):
        return qn.at[c, :, pl.ds(pl.multiple_of(tz * group + ty * unit, 128), unit)]

    place(y, z)[...] = value
    z_copies = {d: send(place(y, z), place(y, z), az_sem, (d,), z_peer[d]) for d in FAR}
    y_copies = {}
    for d in [0] + NEAR:
        tz = lax.rem(z - d + NZ, NZ)
        if d:
            z_copies[d].wait_recv()
        y_copies[d] = [send(place(y, tz), place(y, tz), ay_sem, (d, dy), xy_peer[0, dy]) for dy in DYS]
    c_copies = {}
    for d in [0] + NEAR:
        for copy in y_copies[d]:
            copy.wait_recv()
        tz = lax.rem(z - d + NZ, NZ)
        span = qn.at[c, :, pl.ds(pl.multiple_of(tz * group, 128), group)]
        c_copies[d] = send(span, span, ac_sem, (d,), other)
    outs = []
    for d in [0] + NEAR:
        c_copies[d].wait_recv()
        tz = lax.rem(z - d + NZ, NZ)
        s = pl.ds(pl.multiple_of(tz * group, 128), group)
        copy = pltpu.make_async_copy(qn.at[:, :, s], qn_out.at[:, :, s], out_sem.at[d])
        copy.start()
        outs.append(copy)
    for copy in outs:
        copy.wait()
    for copy in pending:
        copy.wait_send()


def residual_kernel(pt_ref, q_ref, g_ref, e_ref, pt_out, q_out, r_out, pstack):
    @pl.when(pl.program_id(0) == 0)
    def _():
        pt_out[...] = pt_ref[...]
        p1, p2 = parts_of(pt_ref[...].T, 2)
        pstack[...] = jnp.concatenate([p1, p1, p2, p2], axis=1)

    q = q_ref[...]
    q_out[...] = q
    q1, q2 = parts_of(q, 2)
    update = jnp.dot(pstack[...], jnp.concatenate([q1, q2, q1, q2], axis=0), preferred_element_type=F32)
    merged = g_ref[0].astype(F32) + e_ref[0].astype(F32)
    r_out[0] = (merged - update).astype(BF16)


def shards(gradient, error_buffer, q_prev):
    _, rows, cols = gradient.shape
    rank = q_prev.shape[0]
    half = rank // NC
    unit = cols // (NY * NZ)
    group = NY * unit
    dma = pltpu.SemaphoreType.DMA
    vmem = pltpu.VMEM
    anywhere = pl.BlockSpec(memory_space=pl.ANY)
    pt, qn = pl.pallas_call(
        reduce_kernel,
        out_shape=(
            jax.ShapeDtypeStruct((rank, rows), F32),
            jax.ShapeDtypeStruct((NC, half, cols), F32),
        ),
        in_specs=[anywhere] * 3,
        out_specs=(pl.BlockSpec(memory_space=pltpu.VMEM), anywhere),
        scratch_shapes=[
            vmem((2 * rows, cols), BF16),
            vmem((rank, cols), F32),
            vmem((rank, rows), F32),
            vmem((NZ, rank, rows), F32),
            vmem((NX * NY, rank, rows), F32),
            vmem((3, rank, rows), F32),
            vmem((NZ, NC, half, group), F32),
            vmem((NZ, half, group), F32),
            vmem((NZ, NY, half, unit), F32),
            vmem((NZ, NY, half, unit), F32),
            vmem((NZ, half, unit), F32),
            vmem((NZ, half, unit), F32),
            vmem((NC, half, cols), F32),
            dma((NZ, 3)),
            dma((2,)),
            dma((2, NZ)),
            dma((2, NX, NY)),
            dma((2, NZ)),
            dma((2, NZ, NY)),
            dma((2, NZ)),
            dma((2, NZ)),
            dma((2, NZ, NY)),
            dma((2, NZ)),
            dma((NZ,)),
        ],
        compiler_params=pltpu.CompilerParams(
            collective_id=0, has_side_effects=True, vmem_limit_bytes=24 * 1024 * 1024
        ),
        cost_estimate=pl.CostEstimate(flops=2 * 10**8, bytes_accessed=8 * 10**6, transcendentals=0),
        name="reduce_factors",
    )(gradient, error_buffer, q_prev)
    qn = qn.reshape(rank, cols)

    block = cols // 8
    wide = pl.BlockSpec((1, rows, block), lambda i: (0, 0, i))
    tall = pl.BlockSpec((rank, block), lambda i: (0, i))
    whole = pl.BlockSpec((rank, rows), lambda i: (0, 0))
    pt, q_new, residual = pl.pallas_call(
        residual_kernel,
        grid=(cols // block,),
        out_shape=(
            jax.ShapeDtypeStruct((rank, rows), F32),
            jax.ShapeDtypeStruct((rank, cols), F32),
            jax.ShapeDtypeStruct((1, rows, cols), BF16),
        ),
        in_specs=[whole, tall, wide, wide],
        out_specs=(whole, tall, wide),
        scratch_shapes=[vmem((rows, 4 * rank), BF16)],
        compiler_params=pltpu.CompilerParams(vmem_limit_bytes=16 * 1024 * 1024),
        cost_estimate=pl.CostEstimate(flops=2 * 10**8, bytes_accessed=11 * 10**6, transcendentals=0),
        name="residual",
    )(pt, qn, gradient, error_buffer)
    return pt.T, q_new, residual


def solution(mesh):
    return jax.shard_map(
        shards,
        mesh=mesh,
        in_specs=(P("dp", None, "tensor"), P("dp", None, "tensor"), P(None, "tensor")),
        out_specs=(P(), P(None, "tensor"), P("dp", None, "tensor")),
        check_vma=False,
    )
```

time: 362 us -> 59 us (0.16)
  waiting for transfers between devices: 176 us -> 0 us
  blocking collectives: 141 us -> 0 us
  Pallas kernels: 0 us -> 53.2 us
  matrix products: 23 us -> 0 us
  between operations: 14.1 us -> 0.65 us
  other arithmetic: 5.21 us -> 0 us
  local copies, waits for them, and re-layouts: 1.17 us -> 4.9 us
    psum x1 -> x0, waiting for transfers between devices: 176 us -> none  [shards(): q_new = lax.psum(local_q, 'dp') / replicas]
    psum x2 -> x0, blocking collectives: 141 us -> none  [the longest x1 131 us: shards(): p_total = lax.psum(across, 'dp')]
    pallas_call x0 -> x2, Pallas kernels: none -> 53.2 us  [the longest x1 48.5 us: shards(): pl.pallas_call(reduce_kernel, out_shape=(jax.ShapeDtypeStruct((rank, rows...]
    dot_general x4 -> x0, matrix products: 22.8 us -> none  [the longest x1 9.1 us: shards(): update = jnp.dot(p_basis, q_new, precision=PRECISE)]
    another operation x5 -> x0, other arithmetic: 4.02 us -> none  [the longest x3 2.14 us: orthonormal(): factor = jnp.linalg.cholesky(gram_matrix)]
    unnamed x6, local copies, waits for them, and re-layouts: 1.1 us -> 4.9 us
  transfers between devices with their start and end apart: 1 -> 0, of which waited for: 1 -> 0; matrix products, arithmetic and copies ran while one was open for 0% -> 0% of each run, Pallas kernels for 0% -> 0%
where the time goes in v1:
time: 59 us; the launch traced here: 58.8 us
  Pallas kernels  53.2 us (90%)
  local copies, waits for them, and re-layouts  4.9 us (8%)
  between operations  0.65 us (1%)
    pallas_call x1, Pallas kernels, shards(): pl.pallas_call(reduce_kernel, out_shape=(jax.ShapeDtypeStruct((rank, rows...  48.5 us
    unnamed x6, local copies, waits for them, and re-layouts  4.9 us
    pallas_call x1, Pallas kernels, shards(): pl.pallas_call(residual_kernel, grid=(cols // block,), out_shape=(jax.Sha...  4.77 us

profile of v1, /device:TPU:1, one launch (start us, length us, event | category | flops | bytes accessed | tf_op | source)
XLA Modules:
  0.0 58.8 jit_solution(10962696643382023779)
XLA Ops:
  0.6 0.0 copy-start
  0.6 1.9 %copy-done = bf16[1,128,12288]{2,1,0:T(8,128)(2,1)S(1)} copy-done((bf16[1,128,12288]{2,1,0:T(8,128)(2,1)S(1)}, bf16[1,128,12288]{2,1,0:T(8,128)(2,1)}, u32[]{:S(2)}) %copy-start) | copy-done | bytes 3145752
  2.5 0.0 copy-start.1
  2.5 1.9 %copy-done.1 = bf16[1,128,12288]{2,1,0:T(8,128)(2,1)S(1)} copy-done((bf16[1,128,12288]{2,1,0:T(8,128)(2,1)S(1)}, bf16[1,128,12288]{2,1,0:T(8,128)(2,1)}, u32[]{:S(2)}) %copy-start.1) | copy-done | bytes 3145752
  4.4 0.0 copy-start.2
  4.4 1.1 %copy-done.2 = f32[16,12288]{1,0:T(8,128)S(1)} copy-done((f32[16,12288]{1,0:T(8,128)S(1)}, f32[16,12288]{1,0:T(8,128)}, u32[]{:S(2)}) %copy-start.2) | copy-done | bytes 786456
  5.5 48.5 %reduce_factors.1 = (f32[16,128]{1,0:T(8,128)S(1)}, f32[2,8,12288]{2,1,0:T(8,128)S(1)}) custom-call(bf16[1,128,12288]{2,1,0:T(8,128)(2,1)S(1)} %copy-done, bf16[1,128,12288]{2,1,0:T(8,128)(2,1)S(1)} %copy-done.1, f32[16,12288]{1,0:T(8,128)S(1)} %copy-done.2), custom_call_target="tpu_custom_call" | custom-call | flops 200000000 | bytes 8000000 | tf_op jit(solution)/shard_map/reduce_factors/pallas_call | solution.py:236
  54.0 4.8 %residual.1 = (f32[16,128]{1,0:T(8,128)}, f32[16,12288]{1,0:T(8,128)}, bf16[1,128,12288]{2,1,0:T(8,128)(2,1)}) custom-call(f32[16,128]{1,0:T(8,128)S(1)} %get-tuple-element.8.pt_ref, f32[16,12288]{1,0:T(8,128)S(1)} %bitcast.2, bf16[1,128,12288]{2,1,0:T(8,128)(2,1)S(1)} %copy-done, bf16[1,128,12288]{2,1,0:T(8,128)(2,1)S(1)} %copy-done.1), custom_call_target="tpu_custom_call" | custom-call | flops 200000000 | bytes 11000000 | tf_op jit(solution)/shard_map/residual/pallas_call | solution.py:282
Async XLA Ops:
  0.6 1.9 %copy-start = (bf16[1,128,12288]{2,1,0:T(8,128)(2,1)S(1)}, bf16[1,128,12288]{2,1,0:T(8,128)(2,1)}, u32[]{:S(2)}) copy-start(bf16[1,128,12288]{2,1,0:T(8,128)(2,1)} %g_ref.1) | copy-start | bytes 9437188
  2.5 1.9 %copy-start.1 = (bf16[1,128,12288]{2,1,0:T(8,128)(2,1)S(1)}, bf16[1,128,12288]{2,1,0:T(8,128)(2,1)}, u32[]{:S(2)}) copy-start(bf16[1,128,12288]{2,1,0:T(8,128)(2,1)} %e_ref.1) | copy-start | bytes 9437188
  4.4 1.1 %copy-start.2 = (f32[16,12288]{1,0:T(8,128)S(1)}, f32[16,12288]{1,0:T(8,128)}, u32[]{:S(2)}) copy-start(f32[16,12288]{1,0:T(8,128)} %q_hbm.1) | copy-start | bytes 2359300

commit v2 on v1

--- a/solution.py
+++ b/solution.py
@@ -61,9 +61,9 @@
 
 
 def reduce_kernel(
-    g_hbm, e_hbm, q_hbm, pt_out, qn_out,
-    ge, qprev, pcore, pz, pxy, psend, qloc, crecv, hs, yrecv, zs, zrecv, qn,
-    load_sem, pc_sem, pz_sem, pxy_sem, c_sem, y_sem, z_sem, az_sem, ay_sem, ac_sem, out_sem,
+    g_hbm, e_hbm, q_hbm, pt_out, qn, ge,
+    qprev, pcore, pz, pxy, psend, qloc, crecv, hs, yrecv, zs, zrecv,
+    load_sem, pc_sem, pz_sem, pxy_sem, c_sem, y_sem, z_sem, az_sem, ay_sem, ac_sem,
 ):
     x, y, z, c = position()
     cols = q_hbm.shape[1]
@@ -195,33 +195,35 @@
         tz = lax.rem(z - d + NZ, NZ)
         span = qn.at[c, :, pl.ds(pl.multiple_of(tz * group, 128), group)]
         c_copies[d] = send(span, span, ac_sem, (d,), other)
-    outs = []
     for d in [0] + NEAR:
         c_copies[d].wait_recv()
-        tz = lax.rem(z - d + NZ, NZ)
-        s = pl.ds(pl.multiple_of(tz * group, 128), group)
-        copy = pltpu.make_async_copy(qn.at[:, :, s], qn_out.at[:, :, s], out_sem.at[d])
-        copy.start()
-        outs.append(copy)
-    for copy in outs:
-        copy.wait()
     for copy in pending:
         copy.wait_send()
 
 
-def residual_kernel(pt_ref, q_ref, g_ref, e_ref, pt_out, q_out, r_out, pstack):
-    @pl.when(pl.program_id(0) == 0)
-    def _():
-        pt_out[...] = pt_ref[...]
-        p1, p2 = parts_of(pt_ref[...].T, 2)
-        pstack[...] = jnp.concatenate([p1, p1, p2, p2], axis=1)
-
-    q = q_ref[...]
-    q_out[...] = q
-    q1, q2 = parts_of(q, 2)
-    update = jnp.dot(pstack[...], jnp.concatenate([q1, q2, q1, q2], axis=0), preferred_element_type=F32)
-    merged = g_ref[0].astype(F32) + e_ref[0].astype(F32)
-    r_out[0] = (merged - update).astype(BF16)
+def residual_kernel(pt_ref, q_ref, ge, pt_out, q_out, r_out, held, sem, out_sem):
+    rows, cols = held.shape
+    rank = pt_ref.shape[0]
+    block = cols // NZ
+    copies = [
+        pltpu.make_async_copy(q_ref, q_out, out_sem.at[0]),
+        pltpu.make_async_copy(pt_ref, pt_out, out_sem.at[1]),
+    ]
+    for copy in copies:
+        copy.start()
+    p1, p2 = parts_of(pt_ref[...].T, 2)
+    stack = jnp.concatenate([p1, p1, p2, p2], axis=1)
+    for k in range(NZ):
+        s = pl.ds(k * block, block)
+        q1, q2 = parts_of(q_ref[:, :, s].reshape(rank, block), 2)
+        update = jnp.dot(stack, jnp.concatenate([q1, q2, q1, q2], axis=0), preferred_element_type=F32)
+        merged = ge[pl.ds(0, rows), s].astype(F32) + ge[pl.ds(rows, rows), s].astype(F32)
+        held[:, s] = (merged - update).astype(BF16)
+        copy = pltpu.make_async_copy(held.at[:, s], r_out.at[0, :, s], sem.at[k])
+        copy.start()
+        copies.append(copy)
+    for copy in copies:
+        copy.wait()
 
 
 def shards(gradient, error_buffer, q_prev):
@@ -233,16 +235,17 @@
     dma = pltpu.SemaphoreType.DMA
     vmem = pltpu.VMEM
     anywhere = pl.BlockSpec(memory_space=pl.ANY)
-    pt, qn = pl.pallas_call(
+    inside = pl.BlockSpec(memory_space=pltpu.VMEM)
+    pt, qn, ge = pl.pallas_call(
         reduce_kernel,
         out_shape=(
-            jax.ShapeDtypeStruct((rank, rows), F32),
-            jax.ShapeDtypeStruct((NC, half, cols), F32),
+            vmem((rank, rows), F32),
+            vmem((NC, half, cols), F32),
+            vmem((2 * rows, cols), BF16),
         ),
         in_specs=[anywhere] * 3,
-        out_specs=(pl.BlockSpec(memory_space=pltpu.VMEM), anywhere),
+        out_specs=(inside,) * 3,
         scratch_shapes=[
-            vmem((2 * rows, cols), BF16),
             vmem((rank, cols), F32),
             vmem((rank, rows), F32),
             vmem((NZ, rank, rows), F32),
@@ -254,7 +257,6 @@
             vmem((NZ, NY, half, unit), F32),
             vmem((NZ, half, unit), F32),
             vmem((NZ, half, unit), F32),
-            vmem((NC, half, cols), F32),
             dma((NZ, 3)),
             dma((2,)),
             dma((2, NZ)),
@@ -265,36 +267,29 @@
             dma((2, NZ)),
             dma((2, NZ, NY)),
             dma((2, NZ)),
-            dma((NZ,)),
         ],
         compiler_params=pltpu.CompilerParams(
             collective_id=0, has_side_effects=True, vmem_limit_bytes=24 * 1024 * 1024
         ),
         cost_estimate=pl.CostEstimate(flops=2 * 10**8, bytes_accessed=8 * 10**6, transcendentals=0),
         name="reduce_factors",
-    )(gradient, error_buffer, q_prev)
-    qn = qn.reshape(rank, cols)
-
-    block = cols // 8
-    wide = pl.BlockSpec((1, rows, block), lambda i: (0, 0, i))
-    tall = pl.BlockSpec((rank, block), lambda i: (0, i))
-    whole = pl.BlockSpec((rank, rows), lambda i: (0, 0))
+    )(*[pltpu.with_memory_space_constraint(v, pltpu.HBM) for v in (gradient, error_buffer, q_prev)])
+
     pt, q_new, residual = pl.pallas_call(
         residual_kernel,
-        grid=(cols // block,),
         out_shape=(
             jax.ShapeDtypeStruct((rank, rows), F32),
-            jax.ShapeDtypeStruct((rank, cols), F32),
+            jax.ShapeDtypeStruct((NC, half, cols), F32),
             jax.ShapeDtypeStruct((1, rows, cols), BF16),
         ),
-        in_specs=[whole, tall, wide, wide],
-        out_specs=(whole, tall, wide),
-        scratch_shapes=[vmem((rows, 4 * rank), BF16)],
+        in_specs=[inside] * 3,
+        out_specs=(anywhere,) * 3,
+        scratch_shapes=[vmem((rows, cols), BF16), dma((NZ,)), dma((2,))],
         compiler_params=pltpu.CompilerParams(vmem_limit_bytes=16 * 1024 * 1024),
         cost_estimate=pl.CostEstimate(flops=2 * 10**8, bytes_accessed=11 * 10**6, transcendentals=0),
         name="residual",
-    )(pt, qn, gradient, error_buffer)
-    return pt.T, q_new, residual
+    )(pt, qn, ge)
+    return pt.T, q_new.reshape(rank, cols), residual
 
 
 def solution(mesh):

time: 59 us -> 51.3 us (0.87)
  local copies, waits for them, and re-layouts: 4.9 us -> 0 us
  Pallas kernels: 53.2 us -> 50.6 us
    unnamed x6 -> x0, local copies, waits for them, and re-layouts: 4.9 us -> none
    pallas_call x2, Pallas kernels: 53.2 us -> 50.6 us  [the longest x1 48.2 us: shards(): pl.pallas_call(reduce_kernel, out_shape=(vmem((rank, rows), F32), vmem((N...]
where the time goes in v2:
time: 51.3 us; the launch traced here: 51.2 us
  Pallas kernels  50.6 us (99%)
  between operations  0.64 us (1%)
    pallas_call x1, Pallas kernels, shards(): pl.pallas_call(reduce_kernel, out_shape=(vmem((rank, rows), F32), vmem((N...  48.2 us
    pallas_call x1, Pallas kernels, shards(): pl.pallas_call(residual_kernel, out_shape=(jax.ShapeDtypeStruct((rank, ro...  2.44 us

profile of v2, /device:TPU:1, one launch (start us, length us, event | category | flops | bytes accessed | tf_op | source)
XLA Modules:
  0.0 51.2 jit_solution(6473728943891348923)
XLA Ops:
  0.6 48.2 %reduce_factors.1 = (f32[16,128]{1,0:T(8,128)S(1)}, f32[2,8,12288]{2,1,0:T(8,128)S(1)}, bf16[256,12288]{1,0:T(8,128)(2,1)S(1)}) custom-call(bf16[1,128,12288]{2,1,0:T(8,128)(2,1)} %g_hbm.1, bf16[1,128,12288]{2,1,0:T(8,128)(2,1)} %e_hbm.1, f32[16,12288]{1,0:T(8,128)} %q_hbm.1), custom_call_target="tpu_custom_call" | custom-call | flops 200000000 | bytes 8000000 | tf_op jit(solution)/shard_map/reduce_factors/pallas_call | solution.py:239
  48.8 2.4 %residual.1 = (f32[16,128]{1,0:T(8,128)}, f32[2,8,12288]{2,1,0:T(8,128)}, bf16[1,128,12288]{2,1,0:T(8,128)(2,1)}) custom-call(f32[16,128]{1,0:T(8,128)S(1)} %get-tuple-element.9.pt_ref, f32[2,8,12288]{2,1,0:T(8,128)S(1)} %get-tuple-element.10.q_ref, bf16[256,12288]{1,0:T(8,128)(2,1)S(1)} %get-tuple-element.11.ge), custom_call_target="tpu_custom_call" | custom-call | flops 200000000 | bytes 11000000 | tf_op jit(solution)/shard_map/residual/pallas_call | solution.py:278

commit v3 on v2

v3 whole, which is shorter than its diff:
```python
import functools

import jax
import jax.numpy as jnp
from jax import lax
from jax.experimental import pallas as pl
from jax.experimental.pallas import tpu as pltpu
from jax.sharding import PartitionSpec as P

MESH = pl.DeviceIdType.MESH
F32 = jnp.float32
BF16 = jnp.bfloat16

NX, NY, NZ, NC = 4, 4, 8, 2
FAR = [4, 3, 5, 2, 6, 1, 7]
DIRECT = [1, 7, 0]
STAGED = [4, 3, 5, 2, 6]
DYS = [2, 1, 3]


def position():
    dp, x = lax.axis_index("dp"), lax.axis_index("tensor")
    c = lax.rem(dp, NC)
    z = lax.rem(lax.div(dp, NC), NZ)
    y = lax.div(dp, NC * NZ)
    return x, y, z, c


def device(x, y, z, c):
    return ((y * NZ + z) * NC + c, x)


def parts_of(value, n):
    out = []
    for _ in range(n):
        part = value.astype(BF16)
        out.append(part)
        value = value - part.astype(F32)
    return out


def orthonormal_rows(pt):
    rank = pt.shape[0]
    gram = [
        jnp.broadcast_to(jnp.sum(pt * pt[k : k + 1], axis=1, keepdims=True), pt.shape)
        for k in range(rank)
    ]
    rows = []
    for k in range(rank):
        pivot = gram[k][k : k + 1]
        root = lax.rsqrt(pivot)
        root = root * (1.5 - 0.5 * pivot * root * root)
        factor = gram[k] * root
        basis = pt[k : k + 1] * root
        rows.append(basis)
        pt = pt - factor * basis
        for j in range(k + 1, rank):
            gram[j] = gram[j] - factor * factor[j : j + 1]
    return jnp.concatenate(rows, axis=0)


def reduce_kernel(
    g_hbm, e_hbm, q_hbm, pt_out, qn, ge,
    qprev, psend, pz, pxy, msend, mrecv, mstack, hs, yrecv, zs, zrecv,
    load_sem, pz_sem, pxy_sem, m_sem, y_sem, z_sem, az_sem, ay_sem, ac_sem,
):
    x, y, z, c = position()
    cols = q_hbm.shape[1]
    rows = g_hbm.shape[1]
    rank = q_hbm.shape[0]
    half = rank // NC
    span = cols // NC
    group = span // NZ
    unit = group // 2
    pending = []

    def send(src, dst, sems, index, to):
        copy = pltpu.make_async_remote_copy(
            src_ref=src, dst_ref=dst, send_sem=sems.at[(0,) + index], recv_sem=sems.at[(1,) + index],
            device_id=to, device_id_type=MESH,
        )
        copy.start()
        pending.append(copy)
        return copy

    def peer(dx=0, dy=0, dz=0, dc=0):
        return device(
            lax.rem(x + dx, NX) if dx else x, lax.rem(y + dy, NY) if dy else y,
            lax.rem(z + dz, NZ) if dz else z, 1 - c if dc else c,
        )

    wide = cols // NZ
    loads = []
    for k in range(NZ):
        s = pl.ds(k * wide, wide)
        batch = [
            pltpu.make_async_copy(q_hbm.at[:, s], qprev.at[:, s], load_sem.at[k, 0]),
            pltpu.make_async_copy(g_hbm.at[0, :, s], ge.at[pl.ds(0, rows), s], load_sem.at[k, 1]),
            pltpu.make_async_copy(e_hbm.at[0, :, s], ge.at[pl.ds(rows, rows), s], load_sem.at[k, 2]),
        ]
        for copy in batch:
            copy.start()
        loads.append(batch)

    offsets = [(0, 0, dz, dc) for dz in range(NZ) for dc in range(NC)]
    offsets += [(dx, dy, 0, dc) for dx in range(NX) for dy in range(NY) for dc in range(NC)]
    offsets += [(0, dy, dz, 0) for dy in range(NY) for dz in DIRECT]
    offsets = [o for o in dict.fromkeys(offsets) if o != (0, 0, 0, 0)]
    barrier = pltpu.get_barrier_semaphore()
    for o in offsets:
        pl.semaphore_signal(barrier, inc=1, device_id=peer(*o), device_id_type=MESH)

    total = jnp.zeros((3 * rank, 2 * rows), F32)
    for k in range(NZ):
        for copy in loads[k]:
            copy.wait()
        s = pl.ds(k * wide, wide)
        stack = jnp.concatenate(parts_of(qprev[:, s], 3), axis=0)
        total += lax.dot_general(stack, ge[:, s], (((1,), (1,)), ((), ())), preferred_element_type=F32)
    total = total[:, :rows] + total[:, rows:]
    mine = total[:rank] + total[rank : 2 * rank] + total[2 * rank :]

    pl.semaphore_wait(barrier, len(offsets))

    psend[0] = mine[:half]
    psend[1] = mine[half:]
    slot = z * NC + c
    copies = []
    for d in FAR + [0]:
        if d:
            copies.append(send(psend.at[c], pz.at[slot], pz_sem, (d, 0), peer(dz=d)))
        copies.append(send(psend.at[1 - c], pz.at[slot], pz_sem, (d, 1), peer(dz=d, dc=1)))
    pz[slot] = psend[c]

    m_copies = []
    for k in range(NZ):
        s = pl.ds(pl.multiple_of((1 - c) * span + k * group, 128), group)
        msend[k] = ge[pl.ds(0, rows), s].astype(F32) + ge[pl.ds(rows, rows), s].astype(F32)
        m_copies.append(send(msend.at[k], mrecv.at[k], m_sem, (k,), peer(dc=1)))

    for copy in copies:
        copy.wait_recv()
    mine = pz[0]
    for k in range(1, NZ * NC):
        mine = mine + pz[k]

    psend[2] = mine
    slot = y * NX + x
    order = sorted(
        [(dx, dy) for dx in range(NX) for dy in range(NY)],
        key=lambda d: -(min(d[0], NX - d[0]) + min(d[1], NY - d[1])),
    )
    copies = []
    for dx, dy in order:
        if (dx, dy) != (0, 0):
            copies.append(send(psend.at[2], pxy.at[slot, c], pxy_sem, (dx, dy, 0), peer(dx, dy)))
        copies.append(send(psend.at[2], pxy.at[slot, c], pxy_sem, (dx, dy, 1), peer(dx, dy, dc=1)))
    pxy[slot, c] = mine

    for k in range(NZ):
        m_copies[k].wait_recv()
        s = pl.ds(pl.multiple_of(c * span + k * group, 128), group)
        both = ge[pl.ds(0, rows), s].astype(F32) + ge[pl.ds(rows, rows), s].astype(F32) + mrecv[k]
        for i, part in enumerate(parts_of(both, 3)):
            mstack[k, pl.ds(i * rows, rows)] = part

    for copy in copies:
        copy.wait_recv()
    mine = pxy[0]
    for k in range(1, NX * NY):
        mine = mine + pxy[k]

    basis = orthonormal_rows(mine.reshape(rank, rows))
    pt_out[...] = basis
    stack = jnp.concatenate(parts_of(basis, 3), axis=0)
    stack = jnp.concatenate([stack] * 3, axis=1)

    order = FAR + [0]
    y_copies = {}
    for d in order:
        three = jnp.dot(stack, mstack[lax.rem(z + d, NZ)], preferred_element_type=F32)
        local = three[:rank] + three[rank : 2 * rank] + three[2 * rank :]
        for k in range(NY):
            hs[d, k] = local[k // 2 * half : (k // 2 + 1) * half, k % 2 * unit : (k % 2 + 1) * unit]
        y_copies[d] = [
            send(hs.at[d, lax.rem(y + dy, NY)], yrecv.at[d, dy], y_sem, (d, dy), peer(dy=dy)) for dy in DYS
        ]
    z_copies = []
    for d in order:
        for copy in y_copies[d]:
            copy.wait_recv()
        value = hs[d, y] + yrecv[d, 1] + yrecv[d, 2] + yrecv[d, 3]
        if d:
            zs[d] = value
            z_copies.append(send(zs.at[d], zrecv.at[d], z_sem, (d,), peer(dz=d)))
    for copy in z_copies:
        copy.wait_recv()
    for d in range(1, NZ):
        value = value + zrecv[d]
    value = value * (1.0 / (NY * NZ * NC))

    def place(ty, tz):
        start = c * span + tz * group + lax.rem(ty, 2) * unit
        return qn.at[lax.div(ty, 2), :, pl.ds(pl.multiple_of(start, 128), unit)]

    def forward(d, dy):
        ref = place(lax.rem(y + NY - dy, NY), lax.rem(z + NZ - d, NZ))
        c_copies.append(send(ref, ref, ac_sem, (d, dy), peer(dc=1)))

    own = place(y, z)
    own[...] = value
    c_copies, y_copies, z_copies = [], {}, {}
    for d in STAGED:
        z_copies[d] = send(own, own, az_sem, (d,), peer(dz=d))
    for d in DIRECT:
        for dy in (2, 1, 3, 0):
            if d or dy:
                y_copies[d, dy] = send(own, own, ay_sem, (d, dy), peer(dy=dy, dz=d))
    forward(0, 0)
    for d in STAGED[::-1]:
        z_copies[d].wait_recv()
        ref = place(y, lax.rem(z + NZ - d, NZ))
        for dy in DYS:
            y_copies[d, dy] = send(ref, ref, ay_sem, (d, dy), peer(dy=dy))
        forward(d, 0)
    for d in DIRECT[::-1] + STAGED[::-1]:
        for dy in (0, 1, 3, 2):
            if (d, dy) in y_copies:
                y_copies[d, dy].wait_recv()
                forward(d, dy)
    for copy in c_copies:
        copy.wait_recv()
    for copy in pending:
        copy.wait_send()


def residual_kernel(pt_ref, q_ref, ge, pt_out, q_out, r_out, held, sem, out_sem):
    rows, cols = held.shape
    rank = pt_ref.shape[0]
    block = cols // NZ
    copies = [
        pltpu.make_async_copy(q_ref, q_out, out_sem.at[0]),
        pltpu.make_async_copy(pt_ref, pt_out, out_sem.at[1]),
    ]
    for copy in copies:
        copy.start()
    p1, p2 = parts_of(pt_ref[...].T, 2)
    stack = jnp.concatenate([p1, p1, p2, p2], axis=1)
    for k in range(NZ):
        s = pl.ds(k * block, block)
        q1, q2 = parts_of(q_ref[:, :, s].reshape(rank, block), 2)
        update = jnp.dot(stack, jnp.concatenate([q1, q2, q1, q2], axis=0), preferred_element_type=F32)
        merged = ge[pl.ds(0, rows), s].astype(F32) + ge[pl.ds(rows, rows), s].astype(F32)
        held[:, s] = (merged - update).astype(BF16)
        copy = pltpu.make_async_copy(held.at[:, s], r_out.at[0, :, s], sem.at[k])
        copy.start()
        copies.append(copy)
    for copy in copies:
        copy.wait()


def shards(gradient, error_buffer, q_prev):
    _, rows, cols = gradient.shape
    rank = q_prev.shape[0]
    half = rank // NC
    unit = cols // (NY * NZ)
    group = cols // NC // NZ
    dma = pltpu.SemaphoreType.DMA
    vmem = pltpu.VMEM
    anywhere = pl.BlockSpec(memory_space=pl.ANY)
    inside = pl.BlockSpec(memory_space=pltpu.VMEM)
    pt, qn, ge = pl.pallas_call(
        reduce_kernel,
        out_shape=(
            vmem((rank, rows), F32),
            vmem((NC, half, cols), F32),
            vmem((2 * rows, cols), BF16),
        ),
        in_specs=[anywhere] * 3,
        out_specs=(inside,) * 3,
        scratch_shapes=[
            vmem((rank, cols), F32),
            vmem((3, half, rows), F32),
            vmem((NZ * NC, half, rows), F32),
            vmem((NX * NY, NC, half, rows), F32),
            vmem((NZ, rows, group), F32),
            vmem((NZ, rows, group), F32),
            vmem((NZ, 3 * rows, group), BF16),
            vmem((NZ, NY, half, unit), F32),
            vmem((NZ, NY, half, unit), F32),
            vmem((NZ, half, unit), F32),
            vmem((NZ, half, unit), F32),
            dma((NZ, 3)),
            dma((2, NZ, NC)),
            dma((2, NX, NY, NC)),
            dma((2, NZ)),
            dma((2, NZ, NY)),
            dma((2, NZ)),
            dma((2, NZ)),
            dma((2, NZ, NY)),
            dma((2, NZ, NY)),
        ],
        compiler_params=pltpu.CompilerParams(
            collective_id=0, has_side_effects=True, vmem_limit_bytes=32 * 1024 * 1024
        ),
        cost_estimate=pl.CostEstimate(flops=2 * 10**8, bytes_accessed=8 * 10**6, transcendentals=0),
        name="reduce_factors",
    )(*[pltpu.with_memory_space_constraint(v, pltpu.HBM) for v in (gradient, error_buffer, q_prev)])

    pt, q_new, residual = pl.pallas_call(
        residual_kernel,
        out_shape=(
            jax.ShapeDtypeStruct((rank, rows), F32),
            jax.ShapeDtypeStruct((NC, half, cols), F32),
            jax.ShapeDtypeStruct((1, rows, cols), BF16),
        ),
        in_specs=[inside] * 3,
        out_specs=(anywhere,) * 3,
        scratch_shapes=[vmem((rows, cols), BF16), dma((NZ,)), dma((2,))],
        compiler_params=pltpu.CompilerParams(vmem_limit_bytes=16 * 1024 * 1024),
        cost_estimate=pl.CostEstimate(flops=2 * 10**8, bytes_accessed=11 * 10**6, transcendentals=0),
        name="residual",
    )(pt, qn, ge)
    return pt.T, q_new.reshape(rank, cols), residual


def solution(mesh):
    return jax.shard_map(
        shards,
        mesh=mesh,
        in_specs=(P("dp", None, "tensor"), P("dp", None, "tensor"), P(None, "tensor")),
        out_specs=(P(), P(None, "tensor"), P("dp", None, "tensor")),
        check_vma=False,
    )
```

time: 51.3 us -> 48.6 us (0.947)
  Pallas kernels: 50.6 us -> 47.9 us
    pallas_call x1, Pallas kernels: 48.2 us -> 45.5 us  [shards(): pl.pallas_call(reduce_kernel, out_shape=(vmem((rank, rows), F32), vmem((N...]
where the time goes in v3:
time: 48.6 us; the launch traced here: 48.5 us
  Pallas kernels  47.9 us (99%)
  between operations  0.64 us (1%)
    pallas_call x1, Pallas kernels, shards(): pl.pallas_call(reduce_kernel, out_shape=(vmem((rank, rows), F32), vmem((N...  45.5 us
    pallas_call x1, Pallas kernels, shards(): pl.pallas_call(residual_kernel, out_shape=(jax.ShapeDtypeStruct((rank, ro...  2.44 us

profile of v3, /device:TPU:1, one launch (start us, length us, event | category | flops | bytes accessed | tf_op | source)
XLA Modules:
  0.0 48.5 jit_solution(12698846117437245660)
XLA Ops:
  0.6 45.5 %reduce_factors.1 = (f32[16,128]{1,0:T(8,128)S(1)}, f32[2,8,12288]{2,1,0:T(8,128)S(1)}, bf16[256,12288]{1,0:T(8,128)(2,1)S(1)}) custom-call(bf16[1,128,12288]{2,1,0:T(8,128)(2,1)} %g_hbm.1, bf16[1,128,12288]{2,1,0:T(8,128)(2,1)} %e_hbm.1, f32[16,12288]{1,0:T(8,128)} %q_hbm.1), custom_call_target="tpu_custom_call" | custom-call | flops 200000000 | bytes 8000000 | tf_op jit(solution)/shard_map/reduce_factors/pallas_call | solution.py:272
  46.1 2.4 %residual.1 = (f32[16,128]{1,0:T(8,128)}, f32[2,8,12288]{2,1,0:T(8,128)}, bf16[1,128,12288]{2,1,0:T(8,128)(2,1)}) custom-call(f32[16,128]{1,0:T(8,128)S(1)} %get-tuple-element.9.pt_ref, f32[2,8,12288]{2,1,0:T(8,128)S(1)} %get-tuple-element.10.q_ref, bf16[256,12288]{1,0:T(8,128)(2,1)S(1)} %get-tuple-element.11.ge), custom_call_target="tpu_custom_call" | custom-call | flops 200000000 | bytes 11000000 | tf_op jit(solution)/shard_map/residual/pallas_call | solution.py:310

commit v4 on v3

--- a/solution.py
+++ b/solution.py
@@ -16,6 +16,8 @@
 DIRECT = [1, 7, 0]
 STAGED = [4, 3, 5, 2, 6]
 DYS = [2, 1, 3]
+LAST = 4
+LOADS = 6
 
 
 def position():
@@ -62,7 +64,7 @@
 def reduce_kernel(
     g_hbm, e_hbm, q_hbm, pt_out, qn, ge,
     qprev, psend, pz, pxy, msend, mrecv, mstack, hs, yrecv, zs, zrecv,
-    load_sem, pz_sem, pxy_sem, m_sem, y_sem, z_sem, az_sem, ay_sem, ac_sem,
+    load_sem, pz_sem, pxy_sem, m_sem, y_sem, z_sem, az_sem, ay_sem, ac_sem, al_sem,
 ):
     x, y, z, c = position()
     cols = q_hbm.shape[1]
@@ -83,15 +85,20 @@
         pending.append(copy)
         return copy
 
+    def drain():
+        for copy in pending:
+            copy.wait_send()
+        pending.clear()
+
     def peer(dx=0, dy=0, dz=0, dc=0):
         return device(
             lax.rem(x + dx, NX) if dx else x, lax.rem(y + dy, NY) if dy else y,
             lax.rem(z + dz, NZ) if dz else z, 1 - c if dc else c,
         )
 
-    wide = cols // NZ
+    wide = cols // LOADS
     loads = []
-    for k in range(NZ):
+    for k in range(LOADS):
         s = pl.ds(k * wide, wide)
         batch = [
             pltpu.make_async_copy(q_hbm.at[:, s], qprev.at[:, s], load_sem.at[k, 0]),
@@ -110,14 +117,15 @@
     for o in offsets:
         pl.semaphore_signal(barrier, inc=1, device_id=peer(*o), device_id_type=MESH)
 
-    total = jnp.zeros((3 * rank, 2 * rows), F32)
-    for k in range(NZ):
+    total = jnp.zeros((3 * rank, rows), F32)
+    for k in range(LOADS):
         for copy in loads[k]:
             copy.wait()
         s = pl.ds(k * wide, wide)
         stack = jnp.concatenate(parts_of(qprev[:, s], 3), axis=0)
-        total += lax.dot_general(stack, ge[:, s], (((1,), (1,)), ((), ())), preferred_element_type=F32)
-    total = total[:, :rows] + total[:, rows:]
+        for start in (0, rows):
+            part = ge[pl.ds(start, rows), s]
+            total += lax.dot_general(stack, part, (((1,), (1,)), ((), ())), preferred_element_type=F32)
     mine = total[:rank] + total[rank : 2 * rank] + total[2 * rank :]
 
     pl.semaphore_wait(barrier, len(offsets))
@@ -164,6 +172,7 @@
         for i, part in enumerate(parts_of(both, 3)):
             mstack[k, pl.ds(i * rows, rows)] = part
 
+    drain()
     for copy in copies:
         copy.wait_recv()
     mine = pxy[0]
@@ -193,6 +202,7 @@
         if d:
             zs[d] = value
             z_copies.append(send(zs.at[d], zrecv.at[d], z_sem, (d,), peer(dz=d)))
+    drain()
     for copy in z_copies:
         copy.wait_recv()
     for d in range(1, NZ):
@@ -203,9 +213,10 @@
         start = c * span + tz * group + lax.rem(ty, 2) * unit
         return qn.at[lax.div(ty, 2), :, pl.ds(pl.multiple_of(start, 128), unit)]
 
-    def forward(d, dy):
-        ref = place(lax.rem(y + NY - dy, NY), lax.rem(z + NZ - d, NZ))
-        c_copies.append(send(ref, ref, ac_sem, (d, dy), peer(dc=1)))
+    def forward(d):
+        start = c * span + lax.rem(z + NZ - d, NZ) * group
+        ref = qn.at[:, :, pl.ds(pl.multiple_of(start, 128), group)]
+        c_copies.append(send(ref, ref, ac_sem, (d,), peer(dc=1)))
 
     own = place(y, z)
     own[...] = value
@@ -216,22 +227,24 @@
         for dy in (2, 1, 3, 0):
             if d or dy:
                 y_copies[d, dy] = send(own, own, ay_sem, (d, dy), peer(dy=dy, dz=d))
-    forward(0, 0)
     for d in STAGED[::-1]:
         z_copies[d].wait_recv()
         ref = place(y, lax.rem(z + NZ - d, NZ))
         for dy in DYS:
             y_copies[d, dy] = send(ref, ref, ay_sem, (d, dy), peer(dy=dy))
-        forward(d, 0)
+            if d == LAST:
+                c_copies.append(send(ref, ref, al_sem, (dy,), peer(dy=dy, dc=1)))
+        if d == LAST:
+            c_copies.append(send(ref, ref, al_sem, (0,), peer(dc=1)))
     for d in DIRECT[::-1] + STAGED[::-1]:
         for dy in (0, 1, 3, 2):
             if (d, dy) in y_copies:
                 y_copies[d, dy].wait_recv()
-                forward(d, dy)
+        if d != LAST:
+            forward(d)
+    drain()
     for copy in c_copies:
         copy.wait_recv()
-    for copy in pending:
-        copy.wait_send()
 
 
 def residual_kernel(pt_ref, q_ref, ge, pt_out, q_out, r_out, held, sem, out_sem):
@@ -290,7 +303,7 @@
             vmem((NZ, NY, half, unit), F32),
             vmem((NZ, half, unit), F32),
             vmem((NZ, half, unit), F32),
-            dma((NZ, 3)),
+            dma((LOADS, 3)),
             dma((2, NZ, NC)),
             dma((2, NX, NY, NC)),
             dma((2, NZ)),
@@ -298,7 +311,8 @@
             dma((2, NZ)),
             dma((2, NZ)),
             dma((2, NZ, NY)),
-            dma((2, NZ, NY)),
+            dma((2, NZ)),
+            dma((2, NY)),
         ],
         compiler_params=pltpu.CompilerParams(
             collective_id=0, has_side_effects=True, vmem_limit_bytes=32 * 1024 * 1024

time: 48.6 us -> 47.8 us (0.984)
  Pallas kernels: 47.9 us -> 47 us
    pallas_call x1, Pallas kernels: 45.5 us -> 44.6 us  [shards(): pl.pallas_call(reduce_kernel, out_shape=(vmem((rank, rows), F32), vmem((N...]
where the time goes in v4:
time: 47.8 us; the launch traced here: 47.7 us
  Pallas kernels  47 us (98%)
  between operations  0.64 us (1%)
    pallas_call x1, Pallas kernels, shards(): pl.pallas_call(reduce_kernel, out_shape=(vmem((rank, rows), F32), vmem((N...  44.6 us
    pallas_call x1, Pallas kernels, shards(): pl.pallas_call(residual_kernel, out_shape=(jax.ShapeDtypeStruct((rank, ro...  2.44 us

profile of v4, /device:TPU:1, one launch (start us, length us, event | category | flops | bytes accessed | tf_op | source)
XLA Modules:
  0.0 47.7 jit_solution(4495933163986252143)
XLA Ops:
  0.6 44.6 %reduce_factors.1 = (f32[16,128]{1,0:T(8,128)S(1)}, f32[2,8,12288]{2,1,0:T(8,128)S(1)}, bf16[256,12288]{1,0:T(8,128)(2,1)S(1)}) custom-call(bf16[1,128,12288]{2,1,0:T(8,128)(2,1)} %g_hbm.1, bf16[1,128,12288]{2,1,0:T(8,128)(2,1)} %e_hbm.1, f32[16,12288]{1,0:T(8,128)} %q_hbm.1), custom_call_target="tpu_custom_call" | custom-call | flops 200000000 | bytes 8000000 | tf_op jit(solution)/shard_map/reduce_factors/pallas_call | solution.py:285
  45.2 2.4 %residual.1 = (f32[16,128]{1,0:T(8,128)}, f32[2,8,12288]{2,1,0:T(8,128)}, bf16[1,128,12288]{2,1,0:T(8,128)(2,1)}) custom-call(f32[16,128]{1,0:T(8,128)S(1)} %get-tuple-element.9.pt_ref, f32[2,8,12288]{2,1,0:T(8,128)S(1)} %get-tuple-element.10.q_ref, bf16[256,12288]{1,0:T(8,128)(2,1)S(1)} %get-tuple-element.11.ge), custom_call_target="tpu_custom_call" | custom-call | flops 200000000 | bytes 11000000 | tf_op jit(solution)/shard_map/residual/pallas_call | solution.py:324

commit v5 on v4

--- a/solution.py
+++ b/solution.py
@@ -13,11 +13,12 @@
 
 NX, NY, NZ, NC = 4, 4, 8, 2
 FAR = [4, 3, 5, 2, 6, 1, 7]
-DIRECT = [1, 7, 0]
-STAGED = [4, 3, 5, 2, 6]
+DIRECT = [2, 6, 1, 7, 0]
+STAGED = [4, 3, 5]
 DYS = [2, 1, 3]
 LAST = 4
 LOADS = 6
+WRITES = 24
 
 
 def position():
@@ -223,10 +224,9 @@
     c_copies, y_copies, z_copies = [], {}, {}
     for d in STAGED:
         z_copies[d] = send(own, own, az_sem, (d,), peer(dz=d))
-    for d in DIRECT:
-        for dy in (2, 1, 3, 0):
-            if d or dy:
-                y_copies[d, dy] = send(own, own, ay_sem, (d, dy), peer(dy=dy, dz=d))
+    direct = [(d, dy) for d in DIRECT for dy in range(NY) if d or dy]
+    for d, dy in sorted(direct, key=lambda o: -min(o[0], NZ - o[0]) - min(o[1], NY - o[1])):
+        y_copies[d, dy] = send(own, own, ay_sem, (d, dy), peer(dy=dy, dz=d))
     for d in STAGED[::-1]:
         z_copies[d].wait_recv()
         ref = place(y, lax.rem(z + NZ - d, NZ))
@@ -250,7 +250,7 @@
 def residual_kernel(pt_ref, q_ref, ge, pt_out, q_out, r_out, held, sem, out_sem):
     rows, cols = held.shape
     rank = pt_ref.shape[0]
-    block = cols // NZ
+    block = cols // WRITES
     copies = [
         pltpu.make_async_copy(q_ref, q_out, out_sem.at[0]),
         pltpu.make_async_copy(pt_ref, pt_out, out_sem.at[1]),
@@ -259,7 +259,7 @@
         copy.start()
     p1, p2 = parts_of(pt_ref[...].T, 2)
     stack = jnp.concatenate([p1, p1, p2, p2], axis=1)
-    for k in range(NZ):
+    for k in range(WRITES):
         s = pl.ds(k * block, block)
         q1, q2 = parts_of(q_ref[:, :, s].reshape(rank, block), 2)
         update = jnp.dot(stack, jnp.concatenate([q1, q2, q1, q2], axis=0), preferred_element_type=F32)
@@ -330,7 +330,7 @@
         ),
         in_specs=[inside] * 3,
         out_specs=(anywhere,) * 3,
-        scratch_shapes=[vmem((rows, cols), BF16), dma((NZ,)), dma((2,))],
+        scratch_shapes=[vmem((rows, cols), BF16), dma((WRITES,)), dma((2,))],
         compiler_params=pltpu.CompilerParams(vmem_limit_bytes=16 * 1024 * 1024),
         cost_estimate=pl.CostEstimate(flops=2 * 10**8, bytes_accessed=11 * 10**6, transcendentals=0),
         name="residual",

time: 47.8 us -> 47 us (0.983)
  Pallas kernels: 47 us -> 46.3 us
    pallas_call x1, Pallas kernels: 44.6 us -> 43.8 us  [shards(): pl.pallas_call(reduce_kernel, out_shape=(vmem((rank, rows), F32), vmem((N...]
where the time goes in v5:
time: 47 us; the launch traced here: 46.9 us
  Pallas kernels  46.3 us (99%)
  between operations  0.64 us (1%)
    pallas_call x1, Pallas kernels, shards(): pl.pallas_call(reduce_kernel, out_shape=(vmem((rank, rows), F32), vmem((N...  43.8 us
    pallas_call x1, Pallas kernels, shards(): pl.pallas_call(residual_kernel, out_shape=(jax.ShapeDtypeStruct((rank, ro...  2.49 us

profile of v5, /device:TPU:1, one launch (start us, length us, event | category | flops | bytes accessed | tf_op | source)
XLA Modules:
  0.0 46.9 jit_solution(16217690770050137691)
XLA Ops:
  0.6 43.8 %reduce_factors.1 = (f32[16,128]{1,0:T(8,128)S(1)}, f32[2,8,12288]{2,1,0:T(8,128)S(1)}, bf16[256,12288]{1,0:T(8,128)(2,1)S(1)}) custom-call(bf16[1,128,12288]{2,1,0:T(8,128)(2,1)} %g_hbm.1, bf16[1,128,12288]{2,1,0:T(8,128)(2,1)} %e_hbm.1, f32[16,12288]{1,0:T(8,128)} %q_hbm.1), custom_call_target="tpu_custom_call" | custom-call | flops 200000000 | bytes 8000000 | tf_op jit(solution)/shard_map/reduce_factors/pallas_call | solution.py:285
  44.4 2.5 %residual.1 = (f32[16,128]{1,0:T(8,128)}, f32[2,8,12288]{2,1,0:T(8,128)}, bf16[1,128,12288]{2,1,0:T(8,128)(2,1)}) custom-call(f32[16,128]{1,0:T(8,128)S(1)} %get-tuple-element.9.pt_ref, f32[2,8,12288]{2,1,0:T(8,128)S(1)} %get-tuple-element.10.q_ref, bf16[256,12288]{1,0:T(8,128)(2,1)S(1)} %get-tuple-element.11.ge), custom_call_target="tpu_custom_call" | custom-call | flops 200000000 | bytes 11000000 | tf_op jit(solution)/shard_map/residual/pallas_call | solution.py:324

commit v6 on v5

--- a/solution.py
+++ b/solution.py
@@ -75,21 +75,17 @@
     span = cols // NC
     group = span // NZ
     unit = group // 2
-    pending = []
-
     def send(src, dst, sems, index, to):
-        copy = pltpu.make_async_remote_copy(
-            src_ref=src, dst_ref=dst, send_sem=sems.at[(0,) + index], recv_sem=sems.at[(1,) + index],
+        pltpu.make_async_remote_copy(
+            src_ref=src, dst_ref=dst, send_sem=sems.at[0], recv_sem=sems.at[1 + index],
             device_id=to, device_id_type=MESH,
-        )
-        copy.start()
-        pending.append(copy)
-        return copy
-
-    def drain():
-        for copy in pending:
-            copy.wait_send()
-        pending.clear()
+        ).start()
+
+    def take(sem, ref):
+        pltpu.make_async_copy(ref, ref, sem).wait()
+
+    def units(n):
+        return hs.at[pl.ds(0, n // NY)] if n % NY == 0 else hs.at[0, pl.ds(0, n)]
 
     def peer(dx=0, dy=0, dz=0, dc=0):
         return device(
@@ -98,17 +94,15 @@
         )
 
     wide = cols // LOADS
-    loads = []
     for k in range(LOADS):
         s = pl.ds(k * wide, wide)
         batch = [
             pltpu.make_async_copy(q_hbm.at[:, s], qprev.at[:, s], load_sem.at[k, 0]),
             pltpu.make_async_copy(g_hbm.at[0, :, s], ge.at[pl.ds(0, rows), s], load_sem.at[k, 1]),
-            pltpu.make_async_copy(e_hbm.at[0, :, s], ge.at[pl.ds(rows, rows), s], load_sem.at[k, 2]),
+            pltpu.make_async_copy(e_hbm.at[0, :, s], ge.at[pl.ds(rows, rows), s], load_sem.at[k, 1]),
         ]
         for copy in batch:
             copy.start()
-        loads.append(batch)
 
     offsets = [(0, 0, dz, dc) for dz in range(NZ) for dc in range(NC)]
     offsets += [(dx, dy, 0, dc) for dx in range(NX) for dy in range(NY) for dc in range(NC)]
@@ -120,9 +114,9 @@
 
     total = jnp.zeros((3 * rank, rows), F32)
     for k in range(LOADS):
-        for copy in loads[k]:
-            copy.wait()
         s = pl.ds(k * wide, wide)
+        take(load_sem.at[k, 0], qprev.at[:, s])
+        take(load_sem.at[k, 1], ge.at[:, s])
         stack = jnp.concatenate(parts_of(qprev[:, s], 3), axis=0)
         for start in (0, rows):
             part = ge[pl.ds(start, rows), s]
@@ -134,78 +128,72 @@
     psend[0] = mine[:half]
     psend[1] = mine[half:]
     slot = z * NC + c
-    copies = []
     for d in FAR + [0]:
         if d:
-            copies.append(send(psend.at[c], pz.at[slot], pz_sem, (d, 0), peer(dz=d)))
-        copies.append(send(psend.at[1 - c], pz.at[slot], pz_sem, (d, 1), peer(dz=d, dc=1)))
+            send(psend.at[c], pz.at[slot], pz_sem, 0, peer(dz=d))
+        send(psend.at[1 - c], pz.at[slot], pz_sem, 0, peer(dz=d, dc=1))
     pz[slot] = psend[c]
 
-    m_copies = []
     for k in range(NZ):
         s = pl.ds(pl.multiple_of((1 - c) * span + k * group, 128), group)
         msend[k] = ge[pl.ds(0, rows), s].astype(F32) + ge[pl.ds(rows, rows), s].astype(F32)
-        m_copies.append(send(msend.at[k], mrecv.at[k], m_sem, (k,), peer(dc=1)))
-
-    for copy in copies:
-        copy.wait_recv()
+        send(msend.at[k], mrecv.at[k], m_sem, k // 4, peer(dc=1))
+
+    take(pz_sem.at[1], pz.at[pl.ds(0, NZ * NC - 1)])
     mine = pz[0]
     for k in range(1, NZ * NC):
         mine = mine + pz[k]
 
     psend[2] = mine
-    slot = y * NX + x
+    slot = (y * NX + x) * NC + c
     order = sorted(
         [(dx, dy) for dx in range(NX) for dy in range(NY)],
         key=lambda d: -(min(d[0], NX - d[0]) + min(d[1], NY - d[1])),
     )
-    copies = []
     for dx, dy in order:
         if (dx, dy) != (0, 0):
-            copies.append(send(psend.at[2], pxy.at[slot, c], pxy_sem, (dx, dy, 0), peer(dx, dy)))
-        copies.append(send(psend.at[2], pxy.at[slot, c], pxy_sem, (dx, dy, 1), peer(dx, dy, dc=1)))
-    pxy[slot, c] = mine
+            send(psend.at[2], pxy.at[slot], pxy_sem, 0, peer(dx, dy))
+        send(psend.at[2], pxy.at[slot], pxy_sem, 0, peer(dx, dy, dc=1))
+    pxy[slot] = mine
 
     for k in range(NZ):
-        m_copies[k].wait_recv()
+        if k % 4 == 0:
+            take(m_sem.at[1 + k // 4], mrecv.at[pl.ds(k, 4)])
         s = pl.ds(pl.multiple_of(c * span + k * group, 128), group)
         both = ge[pl.ds(0, rows), s].astype(F32) + ge[pl.ds(rows, rows), s].astype(F32) + mrecv[k]
         for i, part in enumerate(parts_of(both, 3)):
             mstack[k, pl.ds(i * rows, rows)] = part
 
-    drain()
-    for copy in copies:
-        copy.wait_recv()
-    mine = pxy[0]
-    for k in range(1, NX * NY):
-        mine = mine + pxy[k]
-
-    basis = orthonormal_rows(mine.reshape(rank, rows))
+    take(pz_sem.at[0], pz.at[pl.ds(0, NZ * NC - 1)])
+    take(pxy_sem.at[0], pxy.at[pl.ds(0, NX * NY * NC - 1)])
+    take(m_sem.at[0], msend)
+    take(pxy_sem.at[1], pxy.at[pl.ds(0, NX * NY * NC - 1)])
+    halves = [pxy[0], pxy[1]]
+    for k in range(NC, NX * NY * NC):
+        halves[k % NC] = halves[k % NC] + pxy[k]
+
+    basis = orthonormal_rows(jnp.concatenate(halves, axis=0))
     pt_out[...] = basis
     stack = jnp.concatenate(parts_of(basis, 3), axis=0)
     stack = jnp.concatenate([stack] * 3, axis=1)
 
     order = FAR + [0]
-    y_copies = {}
     for d in order:
         three = jnp.dot(stack, mstack[lax.rem(z + d, NZ)], preferred_element_type=F32)
         local = three[:rank] + three[rank : 2 * rank] + three[2 * rank :]
         for k in range(NY):
             hs[d, k] = local[k // 2 * half : (k // 2 + 1) * half, k % 2 * unit : (k % 2 + 1) * unit]
-        y_copies[d] = [
-            send(hs.at[d, lax.rem(y + dy, NY)], yrecv.at[d, dy], y_sem, (d, dy), peer(dy=dy)) for dy in DYS
-        ]
-    z_copies = []
+        for dy in DYS:
+            send(hs.at[d, lax.rem(y + dy, NY)], yrecv.at[d, dy], y_sem, d, peer(dy=dy))
     for d in order:
-        for copy in y_copies[d]:
-            copy.wait_recv()
+        take(y_sem.at[1 + d], yrecv.at[d, pl.ds(1, NY - 1)])
         value = hs[d, y] + yrecv[d, 1] + yrecv[d, 2] + yrecv[d, 3]
         if d:
             zs[d] = value
-            z_copies.append(send(zs.at[d], zrecv.at[d], z_sem, (d,), peer(dz=d)))
-    drain()
-    for copy in z_copies:
-        copy.wait_recv()
+            send(zs.at[d], zrecv.at[d], z_sem, 0, peer(dz=d))
+    take(y_sem.at[0], units(NZ * (NY - 1)))
+    take(z_sem.at[0], zs.at[pl.ds(1, NZ - 1)])
+    take(z_sem.at[1], zrecv.at[pl.ds(1, NZ - 1)])
     for d in range(1, NZ):
         value = value + zrecv[d]
     value = value * (1.0 / (NY * NZ * NC))
@@ -217,34 +205,35 @@
     def forward(d):
         start = c * span + lax.rem(z + NZ - d, NZ) * group
         ref = qn.at[:, :, pl.ds(pl.multiple_of(start, 128), group)]
-        c_copies.append(send(ref, ref, ac_sem, (d,), peer(dc=1)))
+        send(ref, ref, ac_sem, 0, peer(dc=1))
 
     own = place(y, z)
     own[...] = value
-    c_copies, y_copies, z_copies = [], {}, {}
     for d in STAGED:
-        z_copies[d] = send(own, own, az_sem, (d,), peer(dz=d))
+        send(own, own, az_sem, STAGED.index(d), peer(dz=d))
     direct = [(d, dy) for d in DIRECT for dy in range(NY) if d or dy]
     for d, dy in sorted(direct, key=lambda o: -min(o[0], NZ - o[0]) - min(o[1], NY - o[1])):
-        y_copies[d, dy] = send(own, own, ay_sem, (d, dy), peer(dy=dy, dz=d))
+        send(own, own, ay_sem, d, peer(dy=dy, dz=d))
     for d in STAGED[::-1]:
-        z_copies[d].wait_recv()
+        take(az_sem.at[1 + STAGED.index(d)], units(1))
         ref = place(y, lax.rem(z + NZ - d, NZ))
         for dy in DYS:
-            y_copies[d, dy] = send(ref, ref, ay_sem, (d, dy), peer(dy=dy))
+            send(ref, ref, ay_sem, d, peer(dy=dy))
             if d == LAST:
-                c_copies.append(send(ref, ref, al_sem, (dy,), peer(dy=dy, dc=1)))
+                send(ref, ref, al_sem, 0, peer(dy=dy, dc=1))
         if d == LAST:
-            c_copies.append(send(ref, ref, al_sem, (0,), peer(dc=1)))
+            send(ref, ref, al_sem, 0, peer(dc=1))
     for d in DIRECT[::-1] + STAGED[::-1]:
-        for dy in (0, 1, 3, 2):
-            if (d, dy) in y_copies:
-                y_copies[d, dy].wait_recv()
+        take(ay_sem.at[1 + d], units(NY if d in DIRECT and d else NY - 1))
         if d != LAST:
             forward(d)
-    drain()
-    for copy in c_copies:
-        copy.wait_recv()
+    many = qn.at[:, :, pl.ds(0, (NZ - 1) * group)]
+    take(az_sem.at[0], units(len(STAGED)))
+    take(ay_sem.at[0], units(len(direct) + len(STAGED) * (NY - 1)))
+    take(al_sem.at[0], units(NY))
+    take(al_sem.at[1], units(NY))
+    take(ac_sem.at[1], many)
+    take(ac_sem.at[0], many)
 
 
 def residual_kernel(pt_ref, q_ref, ge, pt_out, q_out, r_out, held, sem, out_sem):
@@ -265,9 +254,8 @@
         update = jnp.dot(stack, jnp.concatenate([q1, q2, q1, q2], axis=0), preferred_element_type=F32)
         merged = ge[pl.ds(0, rows), s].astype(F32) + ge[pl.ds(rows, rows), s].astype(F32)
         held[:, s] = (merged - update).astype(BF16)
-        copy = pltpu.make_async_copy(held.at[:, s], r_out.at[0, :, s], sem.at[k])
-        copy.start()
-        copies.append(copy)
+        pltpu.make_async_copy(held.at[:, s], r_out.at[0, :, s], sem).start()
+    copies.append(pltpu.make_async_copy(held, r_out.at[0], sem))
     for copy in copies:
         copy.wait()
 
@@ -295,7 +283,7 @@
             vmem((rank, cols), F32),
             vmem((3, half, rows), F32),
             vmem((NZ * NC, half, rows), F32),
-            vmem((NX * NY, NC, half, rows), F32),
+            vmem((NX * NY * NC, half, rows), F32),
             vmem((NZ, rows, group), F32),
             vmem((NZ, rows, group), F32),
             vmem((NZ, 3 * rows, group), BF16),
@@ -303,16 +291,16 @@
             vmem((NZ, NY, half, unit), F32),
             vmem((NZ, half, unit), F32),
             vmem((NZ, half, unit), F32),
-            dma((LOADS, 3)),
-            dma((2, NZ, NC)),
-            dma((2, NX, NY, NC)),
-            dma((2, NZ)),
-            dma((2, NZ, NY)),
-            dma((2, NZ)),
-            dma((2, NZ)),
-            dma((2, NZ, NY)),
-            dma((2, NZ)),
-            dma((2, NY)),
+            dma((LOADS, 2)),
+            dma((2,)),
+            dma((2,)),
+            dma((3,)),
+            dma((1 + NZ,)),
+            dma((2,)),
+            dma((1 + len(STAGED),)),
+            dma((1 + NZ,)),
+            dma((2,)),
+            dma((2,)),
         ],
         compiler_params=pltpu.CompilerParams(
             collective_id=0, has_side_effects=True, vmem_limit_bytes=32 * 1024 * 1024
@@ -330,7 +318,7 @@
         ),
         in_specs=[inside] * 3,
         out_specs=(anywhere,) * 3,
-        scratch_shapes=[vmem((rows, cols), BF16), dma((WRITES,)), dma((2,))],
+        scratch_shapes=[vmem((rows, cols), BF16), dma(()), dma((2,))],
         compiler_params=pltpu.CompilerParams(vmem_limit_bytes=16 * 1024 * 1024),
         cost_estimate=pl.CostEstimate(flops=2 * 10**8, bytes_accessed=11 * 10**6, transcendentals=0),
         name="residual",

time: 47 us -> 44.3 us (0.943)
  Pallas kernels: 46.3 us -> 43.6 us
    pallas_call x1, Pallas kernels: 43.8 us -> 41.3 us  [shards(): pl.pallas_call(reduce_kernel, out_shape=(vmem((rank, rows), F32), vmem((N...]
where the time goes in v6:
time: 44.3 us; the launch traced here: 44.2 us
  Pallas kernels  43.6 us (98%)
  between operations  0.64 us (1%)
    pallas_call x1, Pallas kernels, shards(): pl.pallas_call(reduce_kernel, out_shape=(vmem((rank, rows), F32), vmem((N...  41.3 us
    pallas_call x1, Pallas kernels, shards(): pl.pallas_call(residual_kernel, out_shape=(jax.ShapeDtypeStruct((rank, ro...  2.28 us

profile of v6, /device:TPU:1, one launch (start us, length us, event | category | flops | bytes accessed | tf_op | source)
XLA Modules:
  0.0 44.2 jit_solution(14825545438182719112)
XLA Ops:
  0.6 41.3 %reduce_factors.1 = (f32[16,128]{1,0:T(8,128)S(1)}, f32[2,8,12288]{2,1,0:T(8,128)S(1)}, bf16[256,12288]{1,0:T(8,128)(2,1)S(1)}) custom-call(bf16[1,128,12288]{2,1,0:T(8,128)(2,1)} %g_hbm.1, bf16[1,128,12288]{2,1,0:T(8,128)(2,1)} %e_hbm.1, f32[16,12288]{1,0:T(8,128)} %q_hbm.1), custom_call_target="tpu_custom_call" | custom-call | flops 200000000 | bytes 8000000 | tf_op jit(solution)/shard_map/reduce_factors/pallas_call | solution.py:273
  42.0 2.3 %residual.1 = (f32[16,128]{1,0:T(8,128)}, f32[2,8,12288]{2,1,0:T(8,128)}, bf16[1,128,12288]{2,1,0:T(8,128)(2,1)}) custom-call(f32[16,128]{1,0:T(8,128)S(1)} %get-tuple-element.9.pt_ref, f32[2,8,12288]{2,1,0:T(8,128)S(1)} %get-tuple-element.10.q_ref, bf16[256,12288]{1,0:T(8,128)(2,1)S(1)} %get-tuple-element.11.ge), custom_call_target="tpu_custom_call" | custom-call | flops 200000000 | bytes 11000000 | tf_op jit(solution)/shard_map/residual/pallas_call | solution.py:312

commit v7 on v6

--- a/solution.py
+++ b/solution.py
@@ -150,10 +150,10 @@
         [(dx, dy) for dx in range(NX) for dy in range(NY)],
         key=lambda d: -(min(d[0], NX - d[0]) + min(d[1], NY - d[1])),
     )
-    for dx, dy in order:
-        if (dx, dy) != (0, 0):
-            send(psend.at[2], pxy.at[slot], pxy_sem, 0, peer(dx, dy))
-        send(psend.at[2], pxy.at[slot], pxy_sem, 0, peer(dx, dy, dc=1))
+    for dc in range(NC):
+        for dx, dy in order:
+            if dx or dy or dc:
+                send(psend.at[2], pxy.at[slot], pxy_sem, 0, peer(dx, dy, dc=dc))
     pxy[slot] = mine
 
     for k in range(NZ):

time: 44.3 us -> 44.3 us (level)
  no operation moved by 1% of the time
where the time goes in v7:
time: 44.3 us; the launch traced here: 44.2 us
  Pallas kernels  43.6 us (98%)
  between operations  0.64 us (1%)
    pallas_call x1, Pallas kernels, shards(): pl.pallas_call(reduce_kernel, out_shape=(vmem((rank, rows), F32), vmem((N...  41.3 us
    pallas_call x1, Pallas kernels, shards(): pl.pallas_call(residual_kernel, out_shape=(jax.ShapeDtypeStruct((rank, ro...  2.28 us

profile of v7, /device:TPU:1, one launch (start us, length us, event | category | flops | bytes accessed | tf_op | source)
XLA Modules:
  0.0 44.2 jit_solution(5955811461251140521)
XLA Ops:
  0.6 41.3 %reduce_factors.1 = (f32[16,128]{1,0:T(8,128)S(1)}, f32[2,8,12288]{2,1,0:T(8,128)S(1)}, bf16[256,12288]{1,0:T(8,128)(2,1)S(1)}) custom-call(bf16[1,128,12288]{2,1,0:T(8,128)(2,1)} %g_hbm.1, bf16[1,128,12288]{2,1,0:T(8,128)(2,1)} %e_hbm.1, f32[16,12288]{1,0:T(8,128)} %q_hbm.1), custom_call_target="tpu_custom_call" | custom-call | flops 200000000 | bytes 8000000 | tf_op jit(solution)/shard_map/reduce_factors/pallas_call | solution.py:273
  42.0 2.3 %residual.1 = (f32[16,128]{1,0:T(8,128)}, f32[2,8,12288]{2,1,0:T(8,128)}, bf16[1,128,12288]{2,1,0:T(8,128)(2,1)}) custom-call(f32[16,128]{1,0:T(8,128)S(1)} %get-tuple-element.9.pt_ref, f32[2,8,12288]{2,1,0:T(8,128)S(1)} %get-tuple-element.10.q_ref, bf16[256,12288]{1,0:T(8,128)(2,1)S(1)} %get-tuple-element.11.ge), custom_call_target="tpu_custom_call" | custom-call | flops 200000000 | bytes 11000000 | tf_op jit(solution)/shard_map/residual/pallas_call | solution.py:312
